TPU v7x, 512 devices: a whole 4x8x8 slice. The times are simulated.
512 devices in a mesh: wide: 32 (over z, x), narrow: 16 (over y, core).
Axes of the slice: x: 4, y: 8, z: 8, core: 2. Of those that a mesh axis runs over, the one named last changes fastest.
Arguments:
- embeddings: bfloat16 [262144, 1024], P(('wide', 'narrow')), may hold values from -32 to 32
- valid: int32 [262144], P(('wide', 'narrow')), may hold values from 0 to 1, as said below
Outputs:
- whitened: bfloat16 [262144, 1024], P(('wide', 'narrow'))
Inputs may be any that keep to these rules, and one draw needn't show every extreme that they name: The first row of every aligned block of 16 rows has valid = 1.
All inputs are finite; a program needn't handle non-finite values.
Results may differ from a plain program's by a relative error of at most 0.001.
Values sent between devices are 32-bit elements; how exact they have to be, the bound alone decides.
A program may use at most 64 MiB of HBM per device.

v0:
```python
import jax
import jax.numpy as jnp
from jax import lax
from jax.sharding import PartitionSpec as P


def merged(part, axis, combine):
    gathered = jax.tree.map(lambda a: lax.all_gather(a, axis), part)

    def take(source):
        return jax.tree.map(lambda a: lax.dynamic_index_in_dim(a, source, 0, False), gathered)

    return lax.fori_loop(
        1, lax.axis_size(axis), lambda source, state: combine(state, take(source)), take(0)
    )


def shifted_scatter(gram, count_local, sums_local, center):
    return (
        gram
        - sums_local[:, None] * center[None, :]
        - center[:, None] * sums_local[None, :]
        + count_local * center[:, None] * center[None, :]
    )


def narrow_rows(term):
    return lax.psum_scatter(term, "narrow", scatter_dimension=0, tiled=True)


def on_device(embeddings, valid):
    width = embeddings.shape[1]
    narrow_count = lax.axis_size("narrow")
    row_span = width // narrow_count
    offset = lax.axis_index("narrow") * row_span
    mask_half = valid.astype(jnp.bfloat16)
    count_local = jnp.sum(valid.astype(jnp.float32))
    masked = embeddings * mask_half[:, None]
    gram = lax.dot_general(
        masked, embeddings, (((0,), (0,)), ((), ())), preferred_element_type=jnp.float32
    )
    sums_local = jnp.dot(mask_half[None, :], embeddings, preferred_element_type=jnp.float32)[0]
    group_count, group_sums = lax.psum((count_local, sums_local), "narrow")
    group_center = group_sums / group_count
    term = shifted_scatter(gram, count_local, sums_local, group_center)
    group_rows = narrow_rows(term)

    def pooled(left, right):
        left_count, left_sums, left_rows = left
        right_count, right_sums, right_rows = right
        joined = left_count + right_count
        shifts = left_sums / left_count - right_sums / right_count
        shift_rows = lax.dynamic_slice_in_dim(shifts, offset, row_span, 0)
        extra = left_count * right_count / joined * shift_rows[:, None] * shifts[None, :]
        return (joined, left_sums + right_sums, left_rows + right_rows + extra)

    count, sums, own_rows = merged((group_count, group_sums, group_rows), "wide", pooled)
    center = sums / count
    cov_rows = own_rows / count
    ident_rows = (
        lax.broadcasted_iota(jnp.int32, (row_span, width), 0) + offset
        == lax.broadcasted_iota(jnp.int32, (row_span, width), 1)
    ).astype(jnp.float32)
    diag_block = lax.dynamic_slice_in_dim(cov_rows, offset, row_span, 1)
    trace_part = jnp.sum(jnp.diagonal(diag_block))
    square_part = jnp.sum(cov_rows * cov_rows)
    trace_cov, square_sum = lax.psum((trace_part, square_part), "narrow")
    ridge_add = 0.05 * trace_cov / width + 1e-06
    norm_frob = jnp.sqrt(square_sum + 2.0 * ridge_add * trace_cov + width * ridge_add * ridge_add)
    base_rows = (cov_rows + ridge_add * ident_rows) / norm_frob
    root_rows = (3.0 * ident_rows - base_rows) / 2.0
    root_full = lax.all_gather(root_rows, "narrow", axis=0, tiled=True)
    first = jnp.dot(
        base_rows, root_full, precision=lax.Precision.HIGHEST, preferred_element_type=jnp.float32
    )
    second = jnp.dot(
        first, root_full, precision=lax.Precision.HIGHEST, preferred_element_type=jnp.float32
    )
    factor = (3.0 * ident_rows - second) / 2.0
    root_rows = jnp.dot(
        factor, root_full, precision=lax.Precision.HIGHEST, preferred_element_type=jnp.float32
    )
    centered_x = embeddings.astype(jnp.float32) - center
    product = jnp.dot(
        centered_x,
        lax.all_gather(root_rows, "narrow", axis=0, tiled=True),
        precision=lax.Precision.HIGHEST,
        preferred_element_type=jnp.float32,
    )
    return (product / jnp.sqrt(norm_frob)).astype(jnp.bfloat16)


def solution(mesh):
    in_specs = (P(("wide", "narrow"), None), P(("wide", "narrow")))
    out_specs = P(("wide", "narrow"), None)
    return jax.shard_map(
        on_device, mesh=mesh, in_specs=in_specs, out_specs=out_specs, check_vma=False
    )
```

profile of v0, /device:TPU:1, one launch (start us, length us, event | category | flops | bytes accessed | tf_op | source)
XLA Modules:
  0.0 490.2 jit_solution(10090267257957100686)
XLA Ops:
  7.2 1.3 convert_reduce_fusion
  8.5 1.5 fusion.12
  10.0 30.9 %all-reduce.2 = (f32[]{:T(128)}, f32[1024]{0:T(1024)S(1)}) all-reduce(f32[]{:T(128)} %convert_reduce_fusion, f32[1024]{0:T(1024)S(1)} %bitcast.31), channel_id=1, replica_groups=mesh['wide'=32,'narrow'=16] {'narrow'}, use_global_device_ids=true, to_apply=%region_1.0 | all-reduce | flops 1025 | bytes 8200 | tf_op jit(solution)/shard_map/psum | solution.py:43
  40.8 1.3 broadcast_multiply_fusion
  42.1 5.4 %multiply_add_fusion = f32[1024,1024]{1,0:T(8,128)} fusion(bf16[512,1024]{1,0:T(8,128)(2,1)} %param.4, f32[1024]{0:T(1024)S(1)} %get-tuple-element.284, f32[1024]{0:T(1024)S(1)} %bitcast.32, f32[1024]{0:T(1024)S(1)} %get-tuple-element.285, bf16[512]{0:T(512)(128)(2,1)S(1)} %convert_element_type.15), kind=kOutput, calls=%fused_computation.6 | convolution fusion | flops 1080557568 | bytes 5256192 | tf_op jit(solution)/shard_map/dot_general | solution.py:39
  47.6 62.6 %reduce-scatter.2.cloned.1.call-done = f32[64,1024]{1,0:T(8,128)} async-done(((f32[1024,1024]{1,0:T(8,128)}), f32[64,1024]{1,0:T(8,128)}) %reduce-scatter.2.cloned.1.call-update) | async-done | bytes 262160 | tf_op jit(solution)/shard_map/reduce_scatter | solution.py:28
  110.2 35.0 %all-gather = f32[32768]{0:T(1024)S(1)} all-gather(f32[1024]{0:T(1024)S(1)} %get-tuple-element.281), channel_id=2, replica_groups=mesh['wide'=32,'narrow'=16] {'wide'}, dimensions={0}, use_global_device_ids=true | all-gather | bytes 135168 | tf_op jit(solution)/shard_map/all_gather | solution.py:8
  145.3 1.3 dynamic-slice
  146.6 1.3 dynamic-update-slice
  147.9 59.3 %all-reduce = f32[32]{0:T(128)S(1)} all-reduce(f32[32]{0:T(128)S(1)} %dynamic-update-slice), channel_id=1, replica_groups=mesh['wide'=32,'narrow'=16] {'wide'}, use_global_device_ids=true, to_apply=%add | all-reduce | flops 32 | bytes 256
  207.2 11.9 %all-gather.10.cloned.1.call-done = f32[2048,1024]{1,0:T(8,128)} async-done(((f32[64,1024]{1,0:T(8,128)}), f32[2048,1024]{1,0:T(8,128)}) %all-gather.10.cloned.1.call-update) | async-done | bytes 8388624 | tf_op jit(solution)/shard_map/all_gather | solution.py:8
  220.1 116.4 %while.21 = (s32[]{:T(128)}, f32[]{:T(128)}, f32[1024]{0:T(1024)S(1)}, f32[64,1024]{1,0:T(8,128)S(1)}, f32[32]{0:T(128)S(1)}, /*index=5*/f32[32,1024]{1,0:T(8,12...) while((s32[]{:T(128)}, f32[]{:T(128)}, f32[1024]{0:T(1024)S(1)}, ...), condition=%wide.region_5.6_spmd, body=%wide.region_4.5_spmd.sunk | while | flops 200776 | bytes 816103 | solution.py:13
  222.8 1.0 fusion.24
  226.6 1.0 fusion.24
  230.3 1.0 fusion.24
  234.1 1.0 fusion.24
  237.8 1.0 fusion.24
  241.6 1.0 fusion.24
  245.3 1.0 fusion.24
  249.1 1.0 fusion.24
  252.8 1.0 fusion.24
  256.6 1.0 fusion.24
  260.3 1.0 fusion.24
  264.1 1.0 fusion.24
  267.8 1.0 fusion.24
  271.6 1.0 fusion.24
  275.4 1.0 fusion.24
  279.1 1.0 fusion.24
  282.9 1.0 fusion.24
  286.6 1.0 fusion.24
  290.4 1.0 fusion.24
  294.1 1.0 fusion.24
  297.9 1.0 fusion.24
  301.6 1.0 fusion.24
  305.4 1.0 fusion.24
  309.1 1.0 fusion.24
  312.9 1.0 fusion.24
  316.6 1.0 fusion.24
  320.4 1.0 fusion.24
  331.7 1.0 fusion.24
  335.4 1.0 fusion.24
  338.7 37.7 %all-reduce.1 = (f32[]{:T(128)}, f32[]{:T(128)}) all-reduce(f32[]{:T(128)} %get-tuple-element.282, f32[]{:T(128)} %reduce_sum.28), channel_id=1, replica_groups=mesh['wide'=32,'narrow'=16] {'narrow'}, use_global_device_ids=true, to_apply=%region_9.10 | all-reduce | flops 2 | bytes 16 | tf_op jit(solution)/shard_map/psum | solution.py:67
  379.6 39.5 %all-gather.6.cloned.1.call-done = f32[1024,1024]{1,0:T(8,128)} async-done(((f32[64,1024]{1,0:T(8,128)}), f32[1024,1024]{1,0:T(8,128)}) %all-gather.6.cloned.1.call-update) | async-done | bytes 4194320 | tf_op jit(solution)/shard_map/all_gather | solution.py:72
  419.1 5.0 %fusion.11 = f32[64,1024]{1,0:T(8,128)S(1)} fusion(f32[1024,1024]{1,0:T(8,128)} %all-gather.6.cloned.1.call-done, f32[64,1024]{1,0:T(8,128)S(1)} %get-tuple-element.283, f32[]{:T(128)S(6)} %sqrt.6, f32[]{:T(128)S(6)} %add.145, s32[64]{0:T(128)S(1)} %iota_add_fusion), kind=kOutput, calls=%fused_computation.29 | convolution fusion | flops 805568512 | bytes 4718856 | tf_op jit(solution)/shard_map/dot_general | solution.py:73
  424.2 2.7 fusion.7
  426.8 3.4 fusion.13
  430.2 43.9 %all-gather.8.cloned.1.call-done = f32[1024,1024]{1,0:T(8,128)} async-done(((f32[64,1024]{1,0:T(8,128)}), f32[1024,1024]{1,0:T(8,128)}) %all-gather.8.cloned.1.call-update) | async-done | bytes 4194320 | tf_op jit(solution)/shard_map/all_gather | solution.py:86
  474.1 9.6 %divide_convert_fusion = bf16[512,1024]{1,0:T(8,128)(2,1)} fusion(f32[1024,1024]{1,0:T(8,128)} %all-gather.8.cloned.1.call-done, bf16[512,1024]{1,0:T(8,128)(2,1)S(1)} %copy-done.1, f32[]{:T(128)S(6)} %sqrt.7, f32[1024]{0:T(1024)S(1)} %broadcast_divide_fusion.1), kind=kOutput, calls=%fused_computation.7 | convolution fusion | flops 6444548096 | bytes 6295556 | tf_op jit(solution)/shard_map/dot_general | solution.py:84
  (152 shorter events, 48.6 us)
Async XLA Ops:
  6.5 103.6 %reduce-scatter.2.cloned.1.call-start = ((), (), s32[]{:S(2)}) async-start(), calls=%async_computation.1 | async-start | bytes 4456448 | tf_op jit(solution)/shard_map/reduce_scatter | solution.py:28
  47.5 171.6 %all-gather.10.cloned.1.call-start = ((), (), s32[]{:S(2)}) async-start(), calls=%async_computation.4 | async-start | bytes 8650752 | tf_op jit(solution)/shard_map/all_gather | solution.py:8
  110.2 308.9 %all-gather.6.cloned.1.call-start = ((), (), s32[]{:S(2)}) async-start(), calls=%async_computation.2 | async-start | bytes 4456448 | tf_op jit(solution)/shard_map/all_gather | solution.py:72
  379.4 94.7 %all-gather.8.cloned.1.call-start = ((), (), s32[]{:S(2)}) async-start(), calls=%async_computation.3 | async-start | bytes 4456448 | tf_op jit(solution)/shard_map/all_gather | solution.py:86
  419.1 5.0 %copy-start = (f32[1024,1024]{1,0:T(8,128)S(1)}, f32[1024,1024]{1,0:T(8,128)}, u32[]{:S(2)}) copy-start(f32[1024,1024]{1,0:T(8,128)} %all-gather.6.cloned.1.call-done) | copy-start | bytes 12582916
  424.1 50.0 %copy-start.1 = (bf16[512,1024]{1,0:T(8,128)(2,1)S(1)}, bf16[512,1024]{1,0:T(8,128)(2,1)}, u32[]{:S(2)}) copy-start(bf16[512,1024]{1,0:T(8,128)(2,1)} %param.4) | copy-start | bytes 3145732
Sparse Core Ops, SparseCore 0:
  47.6 62.4 reduce-scatter.1
  113.3 105.7 all-gather.9
  379.5 39.5 all-gather.5
  430.3 43.7 all-gather.7
where the time goes:
time: 494 us; the launch traced here: 490 us
  blocking collectives  163 us (33%)
  waiting for transfers between devices  158 us (32%)
  other arithmetic  60.5 us (12%)
  loops' own time  42.7 us (9%)
  matrix products  27.4 us (6%)
  local copies, waits for them, and re-layouts  23.1 us (5%)
  between operations  15.4 us (3%)
    reduce_scatter x1, waiting for transfers between devices, narrow_rows(): return lax.psum_scatter(term, 'narrow', scatter_dimension=0, tiled=True)  62.6 us
    unnamed x1, blocking collectives  59.3 us
    all_gather x1, waiting for transfers between devices, on_device(): lax.all_gather(root_rows, 'narrow', axis=0, tiled=True)  43.9 us
    another operation x1, loops' own time, merged(): lax.fori_loop(1, lax.axis_size(axis), lambda source, state: combine(state...  42.7 us
    all_gather x1, waiting for transfers between devices, on_device(): root_full = lax.all_gather(root_rows, 'narrow', axis=0, tiled=True)  39.5 us
    psum x1, blocking collectives, on_device(): trace_cov, square_sum = lax.psum((trace_part, square_part), 'narrow')  37.7 us
    all_gather x1, blocking collectives, merged(): gathered = jax.tree.map(lambda a: lax.all_gather(a, axis), part)  35 us
    add x31, other arithmetic, pooled(): return (joined, left_sums + right_sums, left_rows + right_rows + extra)  32.3 us
  transfers between devices with their start and end apart: 4, of which 4 were waited for; matrix products, arithmetic and copies ran while one was open for 1% of the time, Pallas kernels for 0%

commit v1 on v0

--- a/solution.py
+++ b/solution.py
@@ -2,6 +2,19 @@
 import jax.numpy as jnp
 from jax import lax
 from jax.sharding import PartitionSpec as P
+
+
+def counts_recover(array_here, lane_axis):
+    x_now = jnp.concatenate(
+        lax.all_to_all(
+            jnp.stack([array_here] * lax.axis_size(lane_axis)),
+            axis_name=lane_axis,
+            split_axis=0,
+            concat_axis=0,
+        ),
+        0,
+    )
+    return x_now
 
 
 def merged(part, axis, combine):
@@ -83,7 +96,7 @@
     centered_x = embeddings.astype(jnp.float32) - center
     product = jnp.dot(
         centered_x,
-        lax.all_gather(root_rows, "narrow", axis=0, tiled=True),
+        counts_recover(root_rows, "narrow"),
         precision=lax.Precision.HIGHEST,
         preferred_element_type=jnp.float32,
     )

time: 494 us -> 551 us (1.12)
  waiting for transfers between devices: 158 us -> 208 us
    all_to_all x0 -> x1, waiting for transfers between devices: none -> 93.5 us  [counts_recover(): lax.all_to_all(jnp.stack([array_here] * lax.axis_size(lane_axis)), axis_n...]
    all_gather x1 -> x0, waiting for transfers between devices: 43.9 us -> none  [on_device(): lax.all_gather(root_rows, 'narrow', axis=0, tiled=True)]
  transfers between devices with their start and end apart: 4 -> 4, of which waited for: 4 -> 4; matrix products, arithmetic and copies ran while one was open for 1% -> 0% of each run, Pallas kernels for 0% -> 0%
where the time goes in v1:
time: 551 us; the launch traced here: 547 us
  waiting for transfers between devices  208 us (38%)
  blocking collectives  163 us (30%)
  other arithmetic  60.6 us (11%)
  loops' own time  42.7 us (8%)
  matrix products  26.7 us (5%)
  local copies, waits for them, and re-layouts  25.6 us (5%)
  between operations  15.4 us (3%)
    all_to_all x1, waiting for transfers between devices, counts_recover(): lax.all_to_all(jnp.stack([array_here] * lax.axis_size(lane_axis)), axis_n...  93.5 us
    reduce_scatter x1, waiting for transfers between devices, narrow_rows(): return lax.psum_scatter(term, 'narrow', scatter_dimension=0, tiled=True)  62.5 us
    unnamed x1, blocking collectives  59.2 us
    another operation x1, loops' own time, merged(): lax.fori_loop(1, lax.axis_size(axis), lambda source, state: combine(state...  42.7 us
    all_gather x1, waiting for transfers between devices, on_device(): root_full = lax.all_gather(root_rows, 'narrow', axis=0, tiled=True)  39.9 us
    psum x1, blocking collectives, on_device(): trace_cov, square_sum = lax.psum((trace_part, square_part), 'narrow')  37.6 us
    all_gather x1, blocking collectives, merged(): gathered = jax.tree.map(lambda a: lax.all_gather(a, axis), part)  35.2 us
    add x31, other arithmetic, pooled(): return (joined, left_sums + right_sums, left_rows + right_rows + extra)  32.4 us
  transfers between devices with their start and end apart: 4, of which 4 were waited for; matrix products, arithmetic and copies ran while one was open for 0% of the time, Pallas kernels for 0%

profile of v1, /device:TPU:1, one launch (start us, length us, event | category | flops | bytes accessed | tf_op | source)
XLA Modules:
  0.0 546.9 jit_solution(10098921579468845401)
XLA Ops:
  7.2 1.3 convert_reduce_fusion
  8.5 1.5 fusion.12
  10.0 30.9 %all-reduce.2 = (f32[]{:T(128)}, f32[1024]{0:T(1024)S(1)}) all-reduce(f32[]{:T(128)} %convert_reduce_fusion, f32[1024]{0:T(1024)S(1)} %bitcast.32), channel_id=1, replica_groups=mesh['wide'=32,'narrow'=16] {'narrow'}, use_global_device_ids=true, to_apply=%region_1.0 | all-reduce | flops 1025 | bytes 8200 | tf_op jit(solution)/shard_map/psum | solution.py:56
  40.8 1.3 broadcast_multiply_fusion
  42.1 5.3 multiply_add_fusion
  47.5 62.5 %reduce-scatter.2.cloned.1.call-done = f32[64,1024]{1,0:T(8,128)} async-done(((f32[1024,1024]{1,0:T(8,128)}), f32[64,1024]{1,0:T(8,128)}) %reduce-scatter.2.cloned.1.call-update) | async-done | bytes 262160 | tf_op jit(solution)/shard_map/reduce_scatter | solution.py:41
  110.1 35.2 %all-gather = f32[32768]{0:T(1024)S(1)} all-gather(f32[1024]{0:T(1024)S(1)} %get-tuple-element.281), channel_id=2, replica_groups=mesh['wide'=32,'narrow'=16] {'wide'}, dimensions={0}, use_global_device_ids=true | all-gather | bytes 135168 | tf_op jit(solution)/shard_map/all_gather | solution.py:21
  145.3 1.3 dynamic-slice
  146.6 1.3 dynamic-update-slice
  147.8 59.2 %all-reduce = f32[32]{0:T(128)S(1)} all-reduce(f32[32]{0:T(128)S(1)} %dynamic-update-slice), channel_id=1, replica_groups=mesh['wide'=32,'narrow'=16] {'wide'}, use_global_device_ids=true, to_apply=%add | all-reduce | flops 32 | bytes 256
  207.1 11.9 %all-gather.7.cloned.1.call-done = f32[2048,1024]{1,0:T(8,128)} async-done(((f32[64,1024]{1,0:T(8,128)}), f32[2048,1024]{1,0:T(8,128)}) %all-gather.7.cloned.1.call-update) | async-done | bytes 8388624 | tf_op jit(solution)/shard_map/all_gather | solution.py:21
  220.0 116.5 %while.21 = (s32[]{:T(128)}, f32[]{:T(128)}, f32[1024]{0:T(1024)S(1)}, f32[64,1024]{1,0:T(8,128)S(1)}, f32[32]{0:T(128)S(1)}, /*index=5*/f32[32,1024]{1,0:T(8,12...) while((s32[]{:T(128)}, f32[]{:T(128)}, f32[1024]{0:T(1024)S(1)}, ...), condition=%wide.region_5.6_spmd, body=%wide.region_4.5_spmd.sunk | while | flops 200776 | bytes 816103 | solution.py:26
  222.7 1.0 fusion.24
  226.5 1.0 fusion.24
  230.2 1.0 fusion.24
  234.0 1.0 fusion.24
  237.8 1.0 fusion.24
  241.5 1.0 fusion.24
  245.3 1.0 fusion.24
  249.0 1.0 fusion.24
  252.8 1.0 fusion.24
  256.6 1.0 fusion.24
  260.3 1.0 fusion.24
  264.1 1.0 fusion.24
  267.8 1.0 fusion.24
  271.6 1.0 fusion.24
  275.4 1.0 fusion.24
  279.1 1.0 fusion.24
  282.9 1.0 fusion.24
  286.6 1.0 fusion.24
  290.4 1.0 fusion.24
  294.2 1.0 fusion.24
  297.9 1.0 fusion.24
  301.7 1.0 fusion.24
  313.0 1.0 fusion.24
  316.7 1.0 fusion.24
  324.2 1.0 fusion.24
  328.0 1.0 fusion.24
  335.5 1.0 fusion.24
  338.8 37.6 %all-reduce.1 = (f32[]{:T(128)}, f32[]{:T(128)}) all-reduce(f32[]{:T(128)} %get-tuple-element.282, f32[]{:T(128)} %reduce_sum.28), channel_id=1, replica_groups=mesh['wide'=32,'narrow'=16] {'narrow'}, use_global_device_ids=true, to_apply=%region_9.10 | all-reduce | flops 2 | bytes 16 | tf_op jit(solution)/shard_map/psum | solution.py:80
  379.4 39.9 %all-gather.5.cloned.1.call-done = f32[1024,1024]{1,0:T(8,128)} async-done(((f32[64,1024]{1,0:T(8,128)}), f32[1024,1024]{1,0:T(8,128)}) %all-gather.5.cloned.1.call-update) | async-done | bytes 4194320 | tf_op jit(solution)/shard_map/all_gather | solution.py:85
  419.3 5.0 fusion.11
  424.3 2.6 fusion.7
  427.0 2.6 fusion.13
  429.6 2.5 stack.2
  432.1 5.0 all-to-all-start
  437.2 93.5 %all-to-all-done = f32[16,64,1024]{2,1,0:T(8,128)} async-done(((f32[16,64,1024]{2,1,0:T(8,128)}), f32[16,64,1024]{2,1,0:T(8,128)}, u32[]{:S(2)}, u32[]{:S(2)}) %all-to-all-start) | async-done | bytes 4194336 | tf_op jit(solution)/shard_map/all_to_all | solution.py:9
  530.7 9.6 %divide_convert_fusion = bf16[512,1024]{1,0:T(8,128)(2,1)} fusion(f32[1024,1024]{1,0:T(8,128)} %bitcast.9, bf16[512,1024]{1,0:T(8,128)(2,1)S(1)} %copy-done.1, f32[]{:T(128)S(6)} %sqrt.7, f32[1024]{0:T(1024)S(1)} %broadcast_divide_fusion.1), kind=kOutput, calls=%fused_computation.7 | convolution fusion | flops 6444548096 | bytes 6295556 | tf_op jit(solution)/shard_map/dot_general | solution.py:97
  (152 shorter events, 50.5 us)
Async XLA Ops:
  6.5 103.5 %reduce-scatter.2.cloned.1.call-start = ((), (), s32[]{:S(2)}) async-start(), calls=%async_computation.2 | async-start | bytes 4456448 | tf_op jit(solution)/shard_map/reduce_scatter | solution.py:41
  47.5 171.6 %all-gather.7.cloned.1.call-start = ((), (), s32[]{:S(2)}) async-start(), calls=%async_computation.4 | async-start | bytes 8650752 | tf_op jit(solution)/shard_map/all_gather | solution.py:21
  110.0 309.3 %all-gather.5.cloned.1.call-start = ((), (), s32[]{:S(2)}) async-start(), calls=%async_computation.3 | async-start | bytes 4456448 | tf_op jit(solution)/shard_map/all_gather | solution.py:85
  419.3 5.0 copy-start
  432.1 98.6 %copy-start.1 = (bf16[512,1024]{1,0:T(8,128)(2,1)S(1)}, bf16[512,1024]{1,0:T(8,128)(2,1)}, u32[]{:S(2)}) copy-start(bf16[512,1024]{1,0:T(8,128)(2,1)} %param.4) | copy-start | bytes 3145732
  432.1 98.6 %all-to-all-start = ((f32[16,64,1024]{2,1,0:T(8,128)}), f32[16,64,1024]{2,1,0:T(8,128)}, u32[]{:S(2)}, u32[]{:S(2)}) async-start(f32[16,64,1024]{2,1,0:T(8,128)} %stack.2), calls=%async_computation.1 | async-start | bytes 8388608 | tf_op jit(solution)/shard_map/all_to_all | solution.py:9
Sparse Core Ops, SparseCore 0:
  47.6 62.3 reduce-scatter.1
  113.2 105.8 all-gather.6
  379.5 39.7 all-gather.4
